TPU v7x, 32 devices: a whole 2x2x4 slice. The times are simulated.
32 devices in a mesh: sec: 4 (over y, core), tile: 8 (over z, x).
Axes of the slice: x: 2, y: 2, z: 4, core: 2. Of those that a mesh axis runs over, the one named last changes fastest.
Arguments:
- offsets: float32 [2, 16, 64, 128], P(None, 'sec', 'tile'), may hold values from -6 to 6
- flow_tiles: float32 [16, 1024, 2, 128], P('sec', 'tile'), may hold values from -6 to 6
- confidence: float32 [16, 1024, 128], P('sec', 'tile'), may hold values from 0.1 to 10
- flow_owner: int32 [16, 1024, 1], P('sec', 'tile'), may hold values from 0 to 7; in each aligned block of 128 rows (0 to 127, 128 to 255, ..., all dimensions but the last counted through in order) at most 32 rows name the same one
- flow_row: int32 [16, 1024], P('sec', 'tile'), may hold values from 0 to 7
- match_up: int32 [16, 8, 1024], P('sec', 'tile'), may hold values from 0 to 1023, each once within a row
- match_down: int32 [16, 8, 1024], P('sec', 'tile'), may hold values from 0 to 1023, each once within a row
- classes: int32 [16, 64, 128], P('sec', 'tile'), may hold values from 0 to 3
- spring_table: float32 [2, 4], replicated, may hold values from 0.1 to 1
Outputs:
- position: float32 [2, 16, 64, 128], P(None, 'sec', 'tile')
- velocity: float32 [2, 16, 64, 128], P(None, 'sec', 'tile')
Inputs may be any that keep to these rules, and one draw needn't show every extreme that they name: `flow_owner`: in each aligned block of 128 rows (the flow tiles of one section held by one image owner) no region is named more than 32 times, a bound that some block reaches. `match_up`: each row of 1024 entries names every node of a region once. `match_down`: each row of 1024 entries names every node of a region once.
All inputs are finite; a program needn't handle non-finite values.
Results may differ from a plain program's by a relative error of at most 0.000051.
Values sent between devices are 32-bit elements; how exact they have to be, the bound alone decides.
A program may use at most 64 MiB of HBM per device.

v0:
```python
import jax
import jax.numpy as jnp
from jax import lax
from jax.sharding import PartitionSpec as P

ITERS = 3


def extended(block, sides, width):
    for axis, dim in sides:
        count = lax.axis_size(axis)
        forward = [(i, i + 1) for i in range(count - 1)]
        backward = [(target, source) for source, target in forward]
        low = lax.ppermute(
            lax.slice_in_dim(block, block.shape[dim] - width, None, axis=dim), axis, forward
        )
        high = lax.ppermute(lax.slice_in_dim(block, 0, width, axis=dim), axis, backward)
        block = jnp.concatenate([low, block, high], axis=dim)
    return block


def passed_along(x, axis, by):
    count = lax.axis_size(axis)
    pairs = [(i, i + by) for i in range(count) if 0 <= i + by < count]
    return lax.ppermute(x, axis, pairs)


def stiffness_of(classes, spring_table):
    k_plane = jnp.zeros(classes.shape, jnp.float32)
    k_cross = jnp.zeros(classes.shape, jnp.float32)
    for class_id in range(spring_table.shape[1]):
        class_hit = (classes == class_id).astype(jnp.float32)
        k_plane = k_plane + class_hit * spring_table[0, class_id]
        k_cross = k_cross + class_hit * spring_table[1, class_id]
    return (k_plane, k_cross)


def permute_nodes(source, node_index):
    sec_count = source.shape[1]
    node_count = source.shape[2]
    block_size = 128
    block_count = node_count // block_size
    blocked_index = jnp.moveaxis(node_index.reshape(sec_count, block_count, block_size), 1, 0)
    node_ids = jnp.arange(node_count, dtype=jnp.int32)

    def one_block(block_index):
        one_hot = (block_index[:, :, None] == node_ids[None, None, :]).astype(jnp.float32)
        return jnp.einsum("sbn,csn->csb", one_hot, source, precision=lax.Precision.HIGHEST)

    picked = lax.map(one_block, blocked_index)
    picked = jnp.moveaxis(picked, 0, 2)
    return picked.reshape(source.shape)


def shards(
    offsets,
    flow_tiles,
    confidence,
    flow_owner,
    flow_row,
    match_up,
    match_down,
    classes,
    spring_table,
):
    sec_count = offsets.shape[1]
    row_count = offsets.shape[2]
    col_count = offsets.shape[3]
    owner_count = lax.axis_size("tile")
    flow_count = flow_tiles.shape[1]
    payload = jnp.concatenate(
        [flow_tiles * confidence[:, :, None, :], confidence[:, :, None, :]], axis=2
    )
    payload = payload.reshape(sec_count, flow_count, 3 * col_count)
    target_owner = flow_owner[:, :, 0]
    row_key = target_owner * row_count + flow_row
    picked = (row_key[:, None, :] == jnp.arange(owner_count * row_count)[None, :, None]).astype(
        jnp.float32
    )
    dense_rows = jnp.einsum("skf,sfc->skc", picked, payload, precision=lax.Precision.HIGHEST)
    dense_rows = dense_rows.reshape(sec_count, owner_count, row_count, 3 * col_count)
    own_rows = lax.psum_scatter(dense_rows, "tile", scatter_dimension=1, tiled=True)
    gathered = own_rows.reshape(sec_count, row_count, 3, col_count)
    pulled_sum = jnp.moveaxis(gathered[:, :, :2], 2, 0)
    weight_sum = gathered[:, :, 2]
    k_plane, k_cross = stiffness_of(classes, spring_table)
    up_index = match_up.reshape(sec_count, -1)
    down_index = match_down.reshape(sec_count, -1)
    position = offsets
    velocity = jnp.zeros(offsets.shape, jnp.float32)
    for sweep in range(ITERS):
        padded = extended(position, (("tile", 2),), 1)
        padded = jnp.pad(padded, ((0, 0), (0, 0), (0, 0), (1, 1)))
        laplace = (
            padded[:, :, 2:, 1:-1]
            + padded[:, :, :-2, 1:-1]
            + padded[:, :, 1:-1, 2:]
            + padded[:, :, 1:-1, :-2]
            - 4.0 * position
        )
        next_edge = passed_along(position[:, :1], "sec", -1)
        prev_edge = passed_along(position[:, -1:], "sec", 1)
        above_sec = jnp.concatenate([position[:, 1:], next_edge], axis=1)
        below_sec = jnp.concatenate([prev_edge, position[:, :-1]], axis=1)
        up_pulled = permute_nodes(above_sec.reshape(2, sec_count, -1), up_index).reshape(
            position.shape
        )
        down_pulled = permute_nodes(below_sec.reshape(2, sec_count, -1), down_index).reshape(
            position.shape
        )
        net_force = (
            k_plane * laplace
            + k_cross * (up_pulled + down_pulled - 2.0 * position)
            + (pulled_sum - weight_sum * position) / (1.0 + weight_sum)
        )
        velocity = 0.9 * velocity + 0.5 * net_force
        position = position + 0.5 * velocity
    return (position, velocity)


def solution(mesh):
    placed = (
        P(None, "sec", "tile", None),
        P("sec", "tile", None, None),
        P("sec", "tile", None),
        P("sec", "tile", None),
        P("sec", "tile"),
        P("sec", "tile", None),
        P("sec", "tile", None),
        P("sec", "tile", None),
        P(),
    )
    return jax.shard_map(
        shards,
        mesh=mesh,
        in_specs=placed,
        out_specs=(P(None, "sec", "tile", None), P(None, "sec", "tile", None)),
        check_vma=False,
    )
```

profile of v0, /device:TPU:0, one launch (start us, length us, event | category | flops | bytes accessed | tf_op | source)
XLA Modules:
  0.0 145.1 jit_solution(14757423121345186721)
XLA Ops:
  7.2 1.1 copy.39
  10.8 1.3 collective-permute-start.2
  12.1 3.0 %collective-permute-start.3 = (f32[2,1,8,128]{3,2,1,0:T(8,128)S(1)}, f32[2,1,8,128]{3,2,1,0:T(8,128)S(1)}, u32[]{:S(2)}, u32[]{:S(2)}) collective-permute-start(f32[2,1,8,128]{3,2,1,0:T(8,128)S(1)} %get-tuple-element.345), channel_id=1, source_target_pairs={{0,8},{8,16},{16,24},{1,9},{9,17},{17,25},{2,10},{10,18},{18,26},{... | collective-permute-start | bytes 24584 | tf_op jit(solution)/shard_map/ppermute | solution.py:25
  15.2 1.3 collective-permute-start
  16.5 5.5 %collective-permute-start.1 = (f32[2,4,1,128]{3,2,0,1:T(1,128)S(1)}, f32[2,4,1,128]{3,2,0,1:T(1,128)S(1)}, u32[]{:S(2)}, u32[]{:S(2)}) collective-permute-start(f32[2,4,1,128]{3,2,0,1:T(1,128)S(1)} %get-tuple-element.343), channel_id=1, source_target_pairs={{0,1},{1,2},{2,3},{3,4},{4,5},{5,6},{6,7},{8,9},{9,10},{10,11},{11... | collective-permute-start | bytes 12296 | tf_op jit(solution)/shard_map/ppermute | solution.py:14
  22.7 2.5 %select_add_fusion.1 = (f32[4,8,128]{2,1,0:T(8,128)S(1)}, pred[4,8,128]{2,1,0:T(8,128)(4,1)S(1)}, pred[4,8,128]{2,1,0:T(8,128)(4,1)S(1)}, pred[4,8,128]{2,1,0:T(8,128)(4,1)S(1)}, pred[4,8,128]{2,1,0:T(8,128)(4,1)S(1)}) fusion(f32[]{:T(128)} %bitcast.3, f32[]{:T(128)} %bitcast.2, f32[]{:T(128)} %bitcast.1, f32[]{:T(128)} %bitcast, s32[4,8,128]{2,1,0:T(8,128)S(1)} %copy-done.3), kind=kLoop, calls=%fused_computation.93 | loop fusion | flops 45056 | bytes 49168 | tf_op jit(solution)/shard_map/add | solution.py:33
  25.2 2.5 %select_add_fusion = f32[4,8,128]{2,1,0:T(8,128)S(1)} fusion(pred[4,8,128]{2,1,0:T(8,128)(4,1)S(1)} %get-tuple-element.330, pred[4,8,128]{2,1,0:T(8,128)(4,1)S(1)} %get-tuple-element.329, pred[4,8,128]{2,1,0:T(8,128)(4,1)S(1)} %get-tuple-element.328, pred[4,8,128]{2,1,0:T(8,128)(4,1)S(1)} %get-tuple-element.327, f32[]{:T(128)} %bitcast.7, f32[]{:T(128)} %bitcast.6, ...), kind=kLoop, calls=%fused_computation.92 | loop fusion | flops 28672 | bytes 32784 | tf_op jit(solution)/shard_map/add | solution.py:34
  28.1 9.4 %while.66 = (s32[]{:T(128)}, f32[8,2,4,128]{3,0,1,2:T(8,128)S(1)}, s32[8,4,128]{2,1,0:T(4,128)S(1)}, f32[2,4,1024]{2,0,1:T(2,128)S(1)}, s32[]{:T(128)}, /*index=5*/s32[]{:T(128)}) while((s32[]{:T(128)}, f32[8,2,4,128]{3,0,1,2:T(8,128)S(1)}, s32[8,4,128]{2,1,0:T(4,128)S(1)}, f32[2,4,1024]{2,0,1:T(2,128)S(1)}, s32[]{:T(128)}, ...), condition=%wide.region_1.2_spmd.clone, body=%wide.region_0.0_spmd.clone.sunk | while | flops 13107202 | bytes 51285 | solution.py:50
  32.8 1.1 fusion.83
  33.9 1.1 fusion.83
  37.5 9.4 %while.67 = (s32[]{:T(128)}, f32[8,2,4,128]{3,0,1,2:T(8,128)S(1)}, s32[8,4,128]{2,1,0:T(4,128)S(1)}, f32[2,4,1024]{2,0,1:T(2,128)S(1)}, s32[]{:T(128)}, /*index=5*/s32[]{:T(128)}) while((s32[]{:T(128)}, f32[8,2,4,128]{3,0,1,2:T(8,128)S(1)}, s32[8,4,128]{2,1,0:T(4,128)S(1)}, f32[2,4,1024]{2,0,1:T(2,128)S(1)}, s32[]{:T(128)}, ...), condition=%wide.region_3.4_spmd.clone, body=%wide.region_2.3_spmd.clone.sunk | while | flops 13107202 | bytes 51285 | solution.py:50
  37.5 1.1 fusion.85
  46.9 28.5 %reduce-scatter.2.cloned.1.call-done = f32[4,1,8,384]{3,2,0,1:T(8,128)} async-done(((f32[4,8,8,384]{3,2,0,1:T(8,128)}), f32[4,1,8,384]{3,2,0,1:T(8,128)}) %reduce-scatter.2.cloned.1.call-update) | async-done | bytes 49168 | tf_op jit(solution)/shard_map/reduce_scatter | solution.py:82
  77.7 1.3 collective-permute-start.4
  79.0 4.5 %collective-permute-start.5 = (f32[2,4,1,128]{3,2,0,1:T(1,128)S(1)}, f32[2,4,1,128]{3,2,0,1:T(1,128)S(1)}, u32[]{:S(2)}, u32[]{:S(2)}) collective-permute-start(f32[2,4,1,128]{3,2,0,1:T(1,128)S(1)} %get-tuple-element.337), channel_id=1, source_target_pairs={{0,1},{1,2},{2,3},{3,4},{4,5},{5,6},{6,7},{8,9},{9,10},{10,11},{11... | collective-permute-start | bytes 12296 | tf_op jit(solution)/shard_map/ppermute | solution.py:14
  83.6 1.3 collective-permute-start.6
  84.9 3.0 %collective-permute-start.7 = (f32[2,1,8,128]{3,2,0,1:T(8,128)S(1)}, f32[2,1,8,128]{3,2,0,1:T(8,128)S(1)}, u32[]{:S(2)}, u32[]{:S(2)}) collective-permute-start(f32[2,1,8,128]{3,2,0,1:T(8,128)S(1)} %get-tuple-element.339), channel_id=1, source_target_pairs={{0,8},{8,16},{16,24},{1,9},{9,17},{17,25},{2,10},{10,18},{18,26},{... | collective-permute-start | bytes 24584 | tf_op jit(solution)/shard_map/ppermute | solution.py:25
  88.2 9.4 %while.68 = (s32[]{:T(128)}, f32[8,2,4,128]{3,0,1,2:T(8,128)S(1)}, s32[8,4,128]{2,1,0:T(4,128)S(1)}, f32[2,4,1024]{2,0,1:T(2,128)S(1)}, s32[]{:T(128)}, /*index=5*/s32[]{:T(128)}) while((s32[]{:T(128)}, f32[8,2,4,128]{3,0,1,2:T(8,128)S(1)}, s32[8,4,128]{2,1,0:T(4,128)S(1)}, f32[2,4,1024]{2,0,1:T(2,128)S(1)}, s32[]{:T(128)}, ...), condition=%wide.region_6.7_spmd.clone, body=%wide.region_5.6_spmd.clone.sunk | while | flops 13107202 | bytes 51285 | solution.py:50
  89.4 1.1 fusion.87
  90.5 1.1 fusion.87
  97.6 9.4 %while.69 = (s32[]{:T(128)}, f32[8,2,4,128]{3,0,1,2:T(8,128)S(1)}, s32[8,4,128]{2,1,0:T(4,128)S(1)}, f32[2,4,1024]{2,0,1:T(2,128)S(1)}, s32[]{:T(128)}, /*index=5*/s32[]{:T(128)}) while((s32[]{:T(128)}, f32[8,2,4,128]{3,0,1,2:T(8,128)S(1)}, s32[8,4,128]{2,1,0:T(4,128)S(1)}, f32[2,4,1024]{2,0,1:T(2,128)S(1)}, s32[]{:T(128)}, ...), condition=%wide.region_8.9_spmd.clone, body=%wide.region_7.8_spmd.clone.sunk | while | flops 13107202 | bytes 51285 | solution.py:50
  97.6 1.1 fusion.89
  98.8 1.1 fusion.89
  107.1 1.3 collective-permute-start.8
  108.4 4.8 %collective-permute-start.9 = (f32[2,4,1,128]{3,2,0,1:T(1,128)S(1)}, f32[2,4,1,128]{3,2,0,1:T(1,128)S(1)}, u32[]{:S(2)}, u32[]{:S(2)}) collective-permute-start(f32[2,4,1,128]{3,2,0,1:T(1,128)S(1)} %get-tuple-element.331), channel_id=1, source_target_pairs={{0,1},{1,2},{2,3},{3,4},{4,5},{5,6},{6,7},{8,9},{9,10},{10,11},{11... | collective-permute-start | bytes 12296 | tf_op jit(solution)/shard_map/ppermute | solution.py:14
  113.2 1.3 collective-permute-start.10
  114.5 3.4 %collective-permute-start.11 = (f32[2,1,8,128]{3,2,0,1:T(8,128)S(1)}, f32[2,1,8,128]{3,2,0,1:T(8,128)S(1)}, u32[]{:S(2)}, u32[]{:S(2)}) collective-permute-start(f32[2,1,8,128]{3,2,0,1:T(8,128)S(1)} %get-tuple-element.333), channel_id=1, source_target_pairs={{0,8},{8,16},{16,24},{1,9},{9,17},{17,25},{2,10},{10,18},{18,26},{... | collective-permute-start | bytes 24584 | tf_op jit(solution)/shard_map/ppermute | solution.py:25
  118.1 9.4 %while.70 = (s32[]{:T(128)}, f32[8,2,4,128]{3,0,1,2:T(8,128)S(1)}, s32[8,4,128]{2,1,0:T(4,128)S(1)}, f32[2,4,1024]{2,0,1:T(2,128)S(1)}, s32[]{:T(128)}, /*index=5*/s32[]{:T(128)}) while((s32[]{:T(128)}, f32[8,2,4,128]{3,0,1,2:T(8,128)S(1)}, s32[8,4,128]{2,1,0:T(4,128)S(1)}, f32[2,4,1024]{2,0,1:T(2,128)S(1)}, s32[]{:T(128)}, ...), condition=%wide.region_10.11_spmd.clone, body=%wide.region_9.10_spmd.clone.sunk | while | flops 13107202 | bytes 51285 | solution.py:50
  119.3 1.1 fusion.91
  120.5 1.1 fusion.91
  127.6 9.4 %while.71 = (s32[]{:T(128)}, f32[8,2,4,128]{3,0,1,2:T(8,128)S(1)}, s32[8,4,128]{2,1,0:T(4,128)S(1)}, f32[2,4,1024]{2,0,1:T(2,128)S(1)}, s32[]{:T(128)}, /*index=5*/s32[]{:T(128)}) while((s32[]{:T(128)}, f32[8,2,4,128]{3,0,1,2:T(8,128)S(1)}, s32[8,4,128]{2,1,0:T(4,128)S(1)}, f32[2,4,1024]{2,0,1:T(2,128)S(1)}, s32[]{:T(128)}, ...), condition=%wide.region_12.13_spmd.clone, body=%wide.region_11.12_spmd.clone.sunk | while | flops 13107202 | bytes 51285 | solution.py:50
  127.6 1.1 fusion.93
  (214 shorter events, 51.4 us)
Async XLA Ops:
  7.2 1.2 copy-start.1
  7.2 68.2 %reduce-scatter.2.cloned.1.call-start = ((), (), s32[]{:S(2)}) async-start(), calls=%async_computation.1 | async-start | bytes 442368 | tf_op jit(solution)/shard_map/reduce_scatter | solution.py:82
  8.6 0.7 copy-start.7
  8.6 0.7 copy-start.8
  10.0 0.9 copy-start
  10.0 12.0 %copy-start.6 = (f32[2,4]{1,0:T(2,128)S(1)}, f32[2,4]{1,0:T(2,128)}, u32[]{:S(2)}) copy-start(f32[2,4]{1,0:T(2,128)} %param.29) | copy-start | bytes 100
  10.0 12.7 %copy-start.3 = (s32[4,8,128]{2,1,0:T(8,128)S(1)}, s32[4,8,128]{2,1,0:T(8,128)}, u32[]{:S(2)}) copy-start(s32[4,8,128]{2,1,0:T(8,128)} %param.28) | copy-start | bytes 49156
  10.0 17.7 %copy-start.4 = (s32[4,1,1024]{2,1,0:T(1,128)S(1)}, s32[4,1,1024]{2,1,0:T(1,128)}, u32[]{:S(2)}) copy-start(s32[4,1,1024]{2,1,0:T(1,128)} %param.26) | copy-start | bytes 49156
  10.0 17.8 %copy-start.5 = (s32[4,1,1024]{2,1,0:T(1,128)S(1)}, s32[4,1,1024]{2,1,0:T(1,128)}, u32[]{:S(2)}) copy-start(s32[4,1,1024]{2,1,0:T(1,128)} %param.27) | copy-start | bytes 49156
  10.8 17.1 %collective-permute-start.2 = (f32[2,1,8,128]{3,2,1,0:T(8,128)S(1)}, f32[2,1,8,128]{3,2,1,0:T(8,128)S(1)}, u32[]{:S(2)}, u32[]{:S(2)}) collective-permute-start(f32[2,1,8,128]{3,2,1,0:T(8,128)S(1)} %get-tuple-element.346), channel_id=1, source_target_pairs={{8,0},{16,8},{24,16},{9,1},{17,9},{25,17},{10,2},{18,10},{26,18},{... | collective-permute-start | bytes 24584 | tf_op jit(solution)/shard_map/ppermute | solution.py:25
  12.1 15.8 %collective-permute-start.3 = (f32[2,1,8,128]{3,2,1,0:T(8,128)S(1)}, f32[2,1,8,128]{3,2,1,0:T(8,128)S(1)}, u32[]{:S(2)}, u32[]{:S(2)}) collective-permute-start(f32[2,1,8,128]{3,2,1,0:T(8,128)S(1)} %get-tuple-element.345), channel_id=1, source_target_pairs={{0,8},{8,16},{16,24},{1,9},{9,17},{17,25},{2,10},{10,18},{18,26},{... | collective-permute-start | bytes 24584 | tf_op jit(solution)/shard_map/ppermute | solution.py:25
  15.2 12.6 %collective-permute-start = (f32[2,4,1,128]{3,2,0,1:T(1,128)S(1)}, f32[2,4,1,128]{3,2,0,1:T(1,128)S(1)}, u32[]{:S(2)}, u32[]{:S(2)}) collective-permute-start(f32[2,4,1,128]{3,2,0,1:T(1,128)S(1)} %get-tuple-element.344), channel_id=1, source_target_pairs={{1,0},{2,1},{3,2},{4,3},{5,4},{6,5},{7,6},{9,8},{10,9},{11,10},{12... | collective-permute-start | bytes 12296 | tf_op jit(solution)/shard_map/ppermute | solution.py:17
  16.5 11.3 %collective-permute-start.1 = (f32[2,4,1,128]{3,2,0,1:T(1,128)S(1)}, f32[2,4,1,128]{3,2,0,1:T(1,128)S(1)}, u32[]{:S(2)}, u32[]{:S(2)}) collective-permute-start(f32[2,4,1,128]{3,2,0,1:T(1,128)S(1)} %get-tuple-element.343), channel_id=1, source_target_pairs={{0,1},{1,2},{2,3},{3,4},{4,5},{5,6},{6,7},{8,9},{9,10},{10,11},{11... | collective-permute-start | bytes 12296 | tf_op jit(solution)/shard_map/ppermute | solution.py:14
  77.7 10.2 %collective-permute-start.4 = (f32[2,4,1,128]{3,2,0,1:T(1,128)S(1)}, f32[2,4,1,128]{3,2,0,1:T(1,128)S(1)}, u32[]{:S(2)}, u32[]{:S(2)}) collective-permute-start(f32[2,4,1,128]{3,2,0,1:T(1,128)S(1)} %get-tuple-element.338), channel_id=1, source_target_pairs={{1,0},{2,1},{3,2},{4,3},{5,4},{6,5},{7,6},{9,8},{10,9},{11,10},{12... | collective-permute-start | bytes 12296 | tf_op jit(solution)/shard_map/ppermute | solution.py:17
  79.0 8.9 %collective-permute-start.5 = (f32[2,4,1,128]{3,2,0,1:T(1,128)S(1)}, f32[2,4,1,128]{3,2,0,1:T(1,128)S(1)}, u32[]{:S(2)}, u32[]{:S(2)}) collective-permute-start(f32[2,4,1,128]{3,2,0,1:T(1,128)S(1)} %get-tuple-element.337), channel_id=1, source_target_pairs={{0,1},{1,2},{2,3},{3,4},{4,5},{5,6},{6,7},{8,9},{9,10},{10,11},{11... | collective-permute-start | bytes 12296 | tf_op jit(solution)/shard_map/ppermute | solution.py:14
  83.6 4.5 %collective-permute-start.6 = (f32[2,1,8,128]{3,2,0,1:T(8,128)S(1)}, f32[2,1,8,128]{3,2,0,1:T(8,128)S(1)}, u32[]{:S(2)}, u32[]{:S(2)}) collective-permute-start(f32[2,1,8,128]{3,2,0,1:T(8,128)S(1)} %get-tuple-element.340), channel_id=1, source_target_pairs={{8,0},{16,8},{24,16},{9,1},{17,9},{25,17},{10,2},{18,10},{26,18},{... | collective-permute-start | bytes 24584 | tf_op jit(solution)/shard_map/ppermute | solution.py:25
  84.9 12.6 %collective-permute-start.7 = (f32[2,1,8,128]{3,2,0,1:T(8,128)S(1)}, f32[2,1,8,128]{3,2,0,1:T(8,128)S(1)}, u32[]{:S(2)}, u32[]{:S(2)}) collective-permute-start(f32[2,1,8,128]{3,2,0,1:T(8,128)S(1)} %get-tuple-element.339), channel_id=1, source_target_pairs={{0,8},{8,16},{16,24},{1,9},{9,17},{17,25},{2,10},{10,18},{18,26},{... | collective-permute-start | bytes 24584 | tf_op jit(solution)/shard_map/ppermute | solution.py:25
  97.6 9.4 %copy-start.2 = (f32[4,1,8,384]{3,2,0,1:T(8,128)S(1)}, f32[4,1,8,384]{3,2,0,1:T(8,128)}, u32[]{:S(2)}) copy-start(f32[4,1,8,384]{3,2,0,1:T(8,128)} %reduce-scatter.2.cloned.1.call-done) | copy-start | bytes 147460
  107.1 10.8 %collective-permute-start.8 = (f32[2,4,1,128]{3,2,0,1:T(1,128)S(1)}, f32[2,4,1,128]{3,2,0,1:T(1,128)S(1)}, u32[]{:S(2)}, u32[]{:S(2)}) collective-permute-start(f32[2,4,1,128]{3,2,0,1:T(1,128)S(1)} %get-tuple-element.332), channel_id=1, source_target_pairs={{1,0},{2,1},{3,2},{4,3},{5,4},{6,5},{7,6},{9,8},{10,9},{11,10},{12... | collective-permute-start | bytes 12296 | tf_op jit(solution)/shard_map/ppermute | solution.py:17
  108.4 9.5 %collective-permute-start.9 = (f32[2,4,1,128]{3,2,0,1:T(1,128)S(1)}, f32[2,4,1,128]{3,2,0,1:T(1,128)S(1)}, u32[]{:S(2)}, u32[]{:S(2)}) collective-permute-start(f32[2,4,1,128]{3,2,0,1:T(1,128)S(1)} %get-tuple-element.331), channel_id=1, source_target_pairs={{0,1},{1,2},{2,3},{3,4},{4,5},{5,6},{6,7},{8,9},{9,10},{10,11},{11... | collective-permute-start | bytes 12296 | tf_op jit(solution)/shard_map/ppermute | solution.py:14
  113.2 4.8 %collective-permute-start.10 = (f32[2,1,8,128]{3,2,0,1:T(8,128)S(1)}, f32[2,1,8,128]{3,2,0,1:T(8,128)S(1)}, u32[]{:S(2)}, u32[]{:S(2)}) collective-permute-start(f32[2,1,8,128]{3,2,0,1:T(8,128)S(1)} %get-tuple-element.334), channel_id=1, source_target_pairs={{8,0},{16,8},{24,16},{9,1},{17,9},{25,17},{10,2},{18,10},{26,18},{... | collective-permute-start | bytes 24584 | tf_op jit(solution)/shard_map/ppermute | solution.py:25
  114.5 13.0 %collective-permute-start.11 = (f32[2,1,8,128]{3,2,0,1:T(8,128)S(1)}, f32[2,1,8,128]{3,2,0,1:T(8,128)S(1)}, u32[]{:S(2)}, u32[]{:S(2)}) collective-permute-start(f32[2,1,8,128]{3,2,0,1:T(8,128)S(1)} %get-tuple-element.333), channel_id=1, source_target_pairs={{0,8},{8,16},{16,24},{1,9},{9,17},{17,25},{2,10},{10,18},{18,26},{... | collective-permute-start | bytes 24584 | tf_op jit(solution)/shard_map/ppermute | solution.py:25
Sparse Core Ops, SparseCore 0:
  11.3 64.0 reduce-scatter.1
where the time goes:
time: 147 us; the launch traced here: 145 us
  matrix products  53.3 us (36%)
  starting transfers between devices  32 us (22%)
  waiting for transfers between devices  28.6 us (19%)
  between operations  14.7 us (10%)
  local copies, waits for them, and re-layouts  7.79 us (5%)
  other arithmetic  7.35 us (5%)
    dot_general x48, matrix products, one_block(): jnp.einsum('sbn,csn->csb', one_hot, source, precision=lax.Precision.HIGHEST)  52.6 us
    reduce_scatter x1, waiting for transfers between devices, shards(): lax.psum_scatter(dense_rows, 'tile', scatter_dimension=1, tiled=True)  28.5 us
    ppermute x3, starting transfers between devices, extended(): lax.ppermute(lax.slice_in_dim(block, block.shape[dim] - width, None, axis...  14.8 us
    ppermute x6, starting transfers between devices, passed_along(): return lax.ppermute(x, axis, pairs)  13.3 us
    ppermute x3, starting transfers between devices, extended(): lax.ppermute(lax.slice_in_dim(block, 0, width, axis=dim), axis, backward)  3.88 us
    unnamed x25, local copies, waits for them, and re-layouts  3.22 us
  transfers between devices with their start and end apart: 13, of which 1 were waited for; matrix products, arithmetic and copies ran while one was open for 30% of the time, Pallas kernels for 0%

commit v1 on v0

v1 whole, which is shorter than its diff:
```python
import functools

import jax
import jax.numpy as jnp
from jax import lax
from jax.experimental import pallas as pl
from jax.experimental.pallas import tpu as pltpu
from jax.sharding import PartitionSpec as P

ITERS = 3


def gather_nodes(source, row, col):
    rows = source.shape[0]
    picked = None
    for r in range(rows):
        line = jnp.broadcast_to(source[r : r + 1, :], source.shape)
        taken = jnp.take_along_axis(line, col, axis=1)
        picked = taken if r == 0 else jnp.where(row == r, taken, picked)
    return picked


def kernel(
    n_tile,
    n_sec,
    offsets,
    flow,
    conf,
    owner,
    flow_row,
    match_up,
    match_down,
    classes,
    table,
    pos_out,
    vel_out,
    dense,
    near_other,
    near_own,
    crossing,
    crossed,
    pos,
    vel,
    edge_out,
    edge_in,
    near_send,
    near_recv,
    cross_send,
    cross_recv,
    tile_send,
    tile_recv,
    sec_send,
    sec_recv,
):
    comps, secs, rows, cols = offsets.shape
    flows = conf.shape[1]
    half = n_tile // 2
    t = lax.axis_index("tile")
    s_me = lax.axis_index("sec")
    h, j = t // half, t % half

    barrier = pltpu.get_barrier_semaphore()
    for d in range(1, n_tile):
        pl.semaphore_signal(barrier, inc=1, device_id={"tile": (t + d) % n_tile})
    has_prev, has_next = s_me > 0, s_me < n_sec - 1
    has_left, has_right = t > 0, t < n_tile - 1

    for d in (1, n_sec - 1):
        pl.semaphore_signal(barrier, inc=1, device_id={"sec": (s_me + d) % n_sec})

    zero = jnp.zeros((rows, cols), jnp.float32)
    for s in range(secs):
        for c in range(comps):
            here = offsets[c, s]
            pos[0, s + 1, c] = here
            edge_out[0, 0, c * secs + s : c * secs + s + 1, :] = here[:1]
            edge_out[0, 1, c * secs + s : c * secs + s + 1, :] = here[rows - 1 :]

    key_iota = lax.broadcasted_iota(jnp.int32, (n_tile * rows, flows), 0)
    for s in range(secs):
        key = owner[s : s + 1, :] * rows + flow_row[s : s + 1, :]
        hit = (jnp.broadcast_to(key, key_iota.shape) == key_iota).astype(jnp.float32)
        hit = hit.astype(jnp.bfloat16)
        w = conf[s]
        parts = [w * flow[s, pl.ds(c, flows, stride=comps), :] for c in range(comps)] + [w]
        payload = jnp.concatenate(parts, axis=1)
        high = payload.astype(jnp.bfloat16)
        low = (payload - high.astype(jnp.float32)).astype(jnp.bfloat16)
        both = jnp.concatenate([high, low], axis=0)
        hit2 = jnp.concatenate([hit, hit], axis=1)
        sums = jnp.dot(hit2, both, preferred_element_type=jnp.float32)
        for o in range(n_tile):
            for c in range(comps + 1):
                dense[o, s, c] = sums[o * rows : (o + 1) * rows, c * cols : (c + 1) * cols]

    pl.semaphore_wait(barrier, n_tile + 1)

    def sec_copy(k, up):
        return pltpu.make_async_remote_copy(
            src_ref=pos.at[k, 1 if up else secs],
            dst_ref=pos.at[k, secs + 1 if up else 0],
            send_sem=sec_send.at[k, 0 if up else 1],
            recv_sem=sec_recv.at[k, 0 if up else 1],
            device_id={"sec": s_me - 1 if up else s_me + 1},
        )

    def tile_copy(k, up):
        return pltpu.make_async_remote_copy(
            src_ref=edge_out.at[k, 0 if up else 1],
            dst_ref=edge_in.at[k, 1 if up else 0],
            send_sem=tile_send.at[k, 0 if up else 1],
            recv_sem=tile_recv.at[k, 0 if up else 1],
            device_id={"tile": t - 1 if up else t + 1},
        )

    def near_copy(d, part):
        to = (j + d) % half
        source = dense.at[(1 - h if part == 0 else h) * half + to]
        landing = near_other if part == 0 else near_own
        return pltpu.make_async_remote_copy(
            src_ref=source,
            dst_ref=landing.at[d - 1],
            send_sem=near_send.at[part, d - 1],
            recv_sem=near_recv.at[part, d - 1],
            device_id={"tile": h * half + to},
        )

    cross = pltpu.make_async_remote_copy(
        src_ref=crossing,
        dst_ref=crossed,
        send_sem=cross_send,
        recv_sem=cross_recv,
        device_id={"tile": (1 - h) * half + j},
    )

    def start_halo(k):
        pl.when(has_prev)(lambda: sec_copy(k, True).start())
        pl.when(has_next)(lambda: sec_copy(k, False).start())
        pl.when(has_left)(lambda: tile_copy(k, True).start())
        pl.when(has_right)(lambda: tile_copy(k, False).start())

    def wait_halo(k):
        @pl.when(has_prev)
        def _():
            sec_copy(k, True).wait_send()
            sec_copy(k, False).wait_recv()

        @pl.when(has_next)
        def _():
            sec_copy(k, False).wait_send()
            sec_copy(k, True).wait_recv()

        @pl.when(has_left)
        def _():
            tile_copy(k, True).wait_send()
            tile_copy(k, False).wait_recv()

        @pl.when(has_right)
        def _():
            tile_copy(k, False).wait_send()
            tile_copy(k, True).wait_recv()

    for d in range(1, half):
        near_copy(d, 0).start()
    start_halo(0)

    for k in range(ITERS):

        @pl.when(jnp.logical_not(has_prev))
        def _():
            for c in range(comps):
                pos[k, 0, c] = zero

        @pl.when(jnp.logical_not(has_next))
        def _():
            for c in range(comps):
                pos[k, secs + 1, c] = zero

        @pl.when(jnp.logical_not(has_left))
        def _():
            edge_in[k, 0] = jnp.zeros(edge_in.shape[2:], jnp.float32)

        @pl.when(jnp.logical_not(has_right))
        def _():
            edge_in[k, 1] = jnp.zeros(edge_in.shape[2:], jnp.float32)

    row_iota = lax.broadcasted_iota(jnp.int32, (rows, cols), 0)
    col_iota = lax.broadcasted_iota(jnp.int32, (rows, cols), 1)
    k_plane, k_cross = [], []
    for s in range(secs):
        kind = classes[s]
        plane, across = zero, zero
        for class_id in range(table.shape[1]):
            plane = jnp.where(kind == class_id, table[0, class_id], plane)
            across = jnp.where(kind == class_id, table[1, class_id], across)
        k_plane.append(plane)
        k_cross.append(across)

    def pulled(k, s, c, up):
        index = (match_up if up else match_down)[s]
        source = pos[k, s + 2 if up else s, c]
        return gather_nodes(source, index // cols, index % cols)

    def local_force(k, s, c):
        here = pos[k, s + 1, c]
        west = jnp.where(col_iota == 0, 0.0, pltpu.roll(here, 1, 1))
        east = jnp.where(col_iota == cols - 1, 0.0, pltpu.roll(here, cols - 1, 1))
        north = jnp.where(row_iota == 0, 0.0, pltpu.roll(here, 1, 0))
        south = jnp.where(row_iota == rows - 1, 0.0, pltpu.roll(here, rows - 1, 0))
        force = k_plane[s] * (west + east + north + south - 4.0 * here) - 2.0 * k_cross[s] * here
        if s < secs - 1:
            force = force + k_cross[s] * pulled(k, s, c, True)
        if s > 0:
            force = force + k_cross[s] * pulled(k, s, c, False)
        return force

    def halo_force(k, s, c):
        line = c * secs + s
        north = jnp.where(row_iota == 0, edge_in[k, 0, line : line + 1, :], 0.0)
        south = jnp.where(row_iota == rows - 1, edge_in[k, 1, line : line + 1, :], 0.0)
        force = k_plane[s] * (north + south)
        if s == secs - 1:
            force = force + k_cross[s] * pulled(k, s, c, True)
        if s == 0:
            force = force + k_cross[s] * pulled(k, s, c, False)
        return force

    nodes = [(s, c) for s in [0, secs - 1] + list(range(1, secs - 1)) for c in range(comps)]

    for k in range(ITERS):
        force = {(s, c): local_force(k, s, c) for s, c in nodes}
        if k == 0:
            wait_halo(0)
            force = {(s, c): force[s, c] + halo_force(0, s, c) for s, c in nodes}
            for d in range(1, half):
                near_copy(d, 0).wait_recv()
            for s in range(secs):
                for c in range(comps + 1):
                    total = dense[(1 - h) * half + j, s, c]
                    for d in range(1, half):
                        total = total + near_other[d - 1, s, c]
                    crossing[s, c] = total
            cross.start()
            for d in range(1, half):
                near_copy(d, 1).start()
            for d in range(1, half):
                near_copy(d, 1).wait_recv()
            cross.wait_recv()
            flow_push, flow_hold = {}, {}
            for s in range(secs):
                sums = []
                for c in range(comps + 1):
                    total = dense[t, s, c] + crossed[s, c]
                    for d in range(1, half):
                        total = total + near_own[d - 1, s, c]
                    sums.append(total)
                scale = 1.0 / (1.0 + sums[comps])
                flow_hold[s] = sums[comps] * scale
                for c in range(comps):
                    flow_push[s, c] = sums[c] * scale
        else:
            wait_halo(k)
            force = {(s, c): force[s, c] + halo_force(k, s, c) for s, c in nodes}
        for s, c in nodes:
            here = pos[k, s + 1, c]
            net = force[s, c] + flow_push[s, c] - flow_hold[s] * here
            speed = 0.5 * net if k == 0 else 0.9 * vel[s, c] + 0.5 * net
            moved = here + 0.5 * speed
            if k < ITERS - 1:
                vel[s, c] = speed
                pos[k + 1, s + 1, c] = moved
                line = c * secs + s
                edge_out[k + 1, 0, line : line + 1, :] = moved[:1]
                edge_out[k + 1, 1, line : line + 1, :] = moved[rows - 1 :]
            else:
                vel_out[c, s] = speed
                pos_out[c, s] = moved
        if k < ITERS - 1:
            start_halo(k + 1)
        if k == 0:
            for d in range(1, half):
                near_copy(d, 0).wait_send()
                near_copy(d, 1).wait_send()
            cross.wait_send()


def shards(n_tile, n_sec, *args):
    offsets, flow_tiles, confidence, flow_owner, flow_row = args[:5]
    match_up, match_down, classes, spring_table = args[5:]
    comps, secs, rows, cols = offsets.shape
    flows = confidence.shape[1]
    half = n_tile // 2
    block = (secs, comps + 1, rows, cols)
    vmem = pl.BlockSpec(memory_space=pltpu.VMEM)
    f32 = jnp.float32
    dma = pltpu.SemaphoreType.DMA
    out = jax.ShapeDtypeStruct(offsets.shape, f32)
    return pl.pallas_call(
        functools.partial(kernel, n_tile, n_sec),
        out_shape=(out, out),
        in_specs=[vmem] * 8 + [pl.BlockSpec(memory_space=pltpu.SMEM)],
        out_specs=(vmem, vmem),
        scratch_shapes=[
            pltpu.VMEM((n_tile,) + block, f32),
            pltpu.VMEM((half - 1,) + block, f32),
            pltpu.VMEM((half - 1,) + block, f32),
            pltpu.VMEM(block, f32),
            pltpu.VMEM(block, f32),
            pltpu.VMEM((ITERS, secs + 2, comps, rows, cols), f32),
            pltpu.VMEM((secs, comps, rows, cols), f32),
            pltpu.VMEM((ITERS, 2, comps * secs, cols), f32),
            pltpu.VMEM((ITERS, 2, comps * secs, cols), f32),
            dma((2, half - 1)),
            dma((2, half - 1)),
            dma,
            dma,
            dma((ITERS, 2)),
            dma((ITERS, 2)),
            dma((ITERS, 2)),
            dma((ITERS, 2)),
        ],
        compiler_params=pltpu.CompilerParams(
            collective_id=0, has_side_effects=True, vmem_limit_bytes=32 * 1024 * 1024
        ),
    )(
        offsets,
        flow_tiles.reshape(secs, flows * comps, cols),
        confidence,
        flow_owner.reshape(secs, flows),
        flow_row,
        match_up.reshape(secs, rows, cols),
        match_down.reshape(secs, rows, cols),
        classes,
        spring_table,
    )


def solution(mesh):
    placed = (
        P(None, "sec", "tile", None),
        P("sec", "tile", None, None),
        P("sec", "tile", None),
        P("sec", "tile", None),
        P("sec", "tile"),
        P("sec", "tile", None),
        P("sec", "tile", None),
        P("sec", "tile", None),
        P(),
    )
    return jax.shard_map(
        functools.partial(shards, mesh.shape["tile"], mesh.shape["sec"]),
        mesh=mesh,
        in_specs=placed,
        out_specs=(P(None, "sec", "tile", None), P(None, "sec", "tile", None)),
        check_vma=False,
    )
```

time: 147 us -> 28.7 us (0.20)
  matrix products: 53.3 us -> 0 us
  starting transfers between devices: 32 us -> 0 us
  waiting for transfers between devices: 28.6 us -> 0 us
  Pallas kernels: 0 us -> 20.7 us
  between operations: 14.7 us -> 0.67 us
  other arithmetic: 7.35 us -> 0 us
    dot_general x49 -> x0, matrix products: 53.3 us -> none  [the longest x48 52.6 us: one_block(): jnp.einsum('sbn,csn->csb', one_hot, source, precision=lax.Precision.HIGHEST)]
    ppermute x12 -> x0, starting transfers between devices: 32 us -> none  [the longest x3 14.8 us: extended(): lax.ppermute(lax.slice_in_dim(block, block.shape[dim] - width, None, axis...]
    reduce_scatter x1 -> x0, waiting for transfers between devices: 28.5 us -> none  [shards(): lax.psum_scatter(dense_rows, 'tile', scatter_dimension=1, tiled=True)]
    pallas_call x0 -> x1, Pallas kernels: none -> 20.7 us  [shards(): pl.pallas_call(functools.partial(kernel, n_tile, n_sec), out_shape=(out,...]
    add x7 -> x0, other arithmetic: 6.81 us -> none  [the longest x1 2.54 us: stiffness_of(): k_cross = k_cross + class_hit * spring_table[1, class_id]]
    unnamed x25 -> x20, local copies, waits for them, and re-layouts: 3.22 us -> 6.82 us
    dynamic_update_slice x48 -> x0, local copies, waits for them, and re-layouts: 1.82 us -> none  [permute_nodes(): picked = lax.map(one_block, blocked_index)]
  transfers between devices with their start and end apart: 13 -> 0, of which waited for: 1 -> 0; matrix products, arithmetic and copies ran while one was open for 30% -> 0% of each run, Pallas kernels for 0% -> 0%
where the time goes in v1:
time: 28.7 us; the launch traced here: 28.2 us
  Pallas kernels  20.7 us (72%)
  local copies, waits for them, and re-layouts  6.82 us (24%)
  between operations  0.67 us (2%)
    pallas_call x1, Pallas kernels, shards(): pl.pallas_call(functools.partial(kernel, n_tile, n_sec), out_shape=(out,...  20.7 us
    unnamed x20, local copies, waits for them, and re-layouts  6.82 us

profile of v1, /device:TPU:0, one launch (start us, length us, event | category | flops | bytes accessed | tf_op | source)
XLA Modules:
  0.0 28.2 jit_solution(2202789117501658695)
XLA Ops:
  0.6 0.0 copy-start.7
  0.6 0.0 copy-start.6
  0.7 0.0 copy-start.8
  0.7 0.7 %copy-done.7 = s32[4,128]{1,0:T(4,128)S(1)} copy-done((s32[4,128]{1,0:T(4,128)S(1)}, s32[4,128]{1,0:T(4,128)}, u32[]{:S(2)}) %copy-start.7) | copy-done | bytes 2072
  1.3 0.0 copy-done.6
  1.3 0.0 copy-done.8
  1.3 0.0 copy-start
  1.3 1.0 %copy-done = f32[4,128,2,128]{3,2,1,0:T(2,128)S(1)} copy-done((f32[4,128,2,128]{3,2,1,0:T(2,128)S(1)}, f32[4,128,2,128]{3,2,1,0:T(2,128)}, u32[]{:S(2)}) %copy-start) | copy-done | bytes 524312
  2.4 0.0 copy-start.1
  2.4 0.9 %copy-done.1 = f32[4,128,128]{2,1,0:T(8,128)S(1)} copy-done((f32[4,128,128]{2,1,0:T(8,128)S(1)}, f32[4,128,128]{2,1,0:T(8,128)}, u32[]{:S(2)}) %copy-start.1) | copy-done | bytes 262168
  3.3 0.0 copy-start.2
  3.3 0.8 %copy-done.2 = f32[2,4,8,128]{3,2,1,0:T(8,128)S(1)} copy-done((f32[2,4,8,128]{3,2,1,0:T(8,128)S(1)}, f32[2,4,8,128]{3,2,1,0:T(8,128)}, u32[]{:S(2)}) %copy-start.2) | copy-done | bytes 32792
  4.1 0.0 copy-start.3
  4.1 0.7 %copy-done.3 = s32[4,1,1024]{2,1,0:T(1,128)S(1)} copy-done((s32[4,1,1024]{2,1,0:T(1,128)S(1)}, s32[4,1,1024]{2,1,0:T(1,128)}, u32[]{:S(2)}) %copy-start.3) | copy-done | bytes 16408
  4.8 0.0 copy-start.4
  4.8 0.7 %copy-done.4 = s32[4,1,1024]{2,1,0:T(1,128)S(1)} copy-done((s32[4,1,1024]{2,1,0:T(1,128)S(1)}, s32[4,1,1024]{2,1,0:T(1,128)}, u32[]{:S(2)}) %copy-start.4) | copy-done | bytes 16408
  5.5 0.0 copy-start.5
  5.5 0.7 %copy-done.5 = s32[4,8,128]{2,1,0:T(8,128)S(1)} copy-done((s32[4,8,128]{2,1,0:T(8,128)S(1)}, s32[4,8,128]{2,1,0:T(8,128)}, u32[]{:S(2)}) %copy-start.5) | copy-done | bytes 16408
  6.2 20.7 %shard_map.104 = (f32[2,4,8,128]{3,2,1,0:T(8,128)S(1)}, f32[2,4,8,128]{3,2,1,0:T(8,128)S(1)}) custom-call(f32[2,4,8,128]{3,2,1,0:T(8,128)S(1)} %copy-done.2, f32[4,256,128]{2,1,0:T(8,128)S(1)} %bitcast.4, f32[4,128,128]{2,1,0:T(8,128)S(1)} %copy-done.1, s32[4,128]{1,0:T(4,128)S(1)} %bitcast.7, s32[4,128]{1,0:T(4,128)S(1)} %copy-done.7, ...), custom_call_target="tpu_custom_call" | custom-call | tf_op jit(solution)/shard_map/pallas_call | solution.py:298
  27.0 0.6 %copy.13 = f32[2,4,8,128]{3,2,1,0:T(8,128)} copy(f32[2,4,8,128]{3,2,1,0:T(8,128)S(1)} %get-tuple-element.4) | data formatting | bytes 65536
  27.6 0.6 %copy.14 = f32[2,4,8,128]{3,2,1,0:T(8,128)} copy(f32[2,4,8,128]{3,2,1,0:T(8,128)S(1)} %get-tuple-element.5) | data formatting | bytes 65536
Async XLA Ops:
  0.6 0.7 %copy-start.7 = (s32[4,128]{1,0:T(4,128)S(1)}, s32[4,128]{1,0:T(4,128)}, u32[]{:S(2)}) copy-start(s32[4,128]{1,0:T(4,128)} %flow_row.1) | copy-start | bytes 6148
  0.6 0.7 %copy-start.6 = (s32[4,128,1]{1,2,0:T(1,128)S(1)}, s32[4,128,1]{1,2,0:T(1,128)}, u32[]{:S(2)}) copy-start(s32[4,128,1]{1,2,0:T(1,128)} %param.12) | copy-start | bytes 6148
  0.7 0.7 %copy-start.8 = (f32[2,4]{1,0:T(2,128)S(1)}, f32[2,4]{1,0:T(2,128)}, u32[]{:S(2)}) copy-start(f32[2,4]{1,0:T(2,128)} %table.1) | copy-start | bytes 100
  1.3 1.0 %copy-start = (f32[4,128,2,128]{3,2,1,0:T(2,128)S(1)}, f32[4,128,2,128]{3,2,1,0:T(2,128)}, u32[]{:S(2)}) copy-start(f32[4,128,2,128]{3,2,1,0:T(2,128)} %param.10) | copy-start | bytes 1572868
  2.4 0.9 %copy-start.1 = (f32[4,128,128]{2,1,0:T(8,128)S(1)}, f32[4,128,128]{2,1,0:T(8,128)}, u32[]{:S(2)}) copy-start(f32[4,128,128]{2,1,0:T(8,128)} %conf.1) | copy-start | bytes 786436
  3.3 0.8 %copy-start.2 = (f32[2,4,8,128]{3,2,1,0:T(8,128)S(1)}, f32[2,4,8,128]{3,2,1,0:T(8,128)}, u32[]{:S(2)}) copy-start(f32[2,4,8,128]{3,2,1,0:T(8,128)} %offsets.1) | copy-start | bytes 98308
  4.1 0.7 %copy-start.3 = (s32[4,1,1024]{2,1,0:T(1,128)S(1)}, s32[4,1,1024]{2,1,0:T(1,128)}, u32[]{:S(2)}) copy-start(s32[4,1,1024]{2,1,0:T(1,128)} %param.14) | copy-start | bytes 49156
  4.8 0.7 %copy-start.4 = (s32[4,1,1024]{2,1,0:T(1,128)S(1)}, s32[4,1,1024]{2,1,0:T(1,128)}, u32[]{:S(2)}) copy-start(s32[4,1,1024]{2,1,0:T(1,128)} %param.15) | copy-start | bytes 49156
  5.5 0.7 %copy-start.5 = (s32[4,8,128]{2,1,0:T(8,128)S(1)}, s32[4,8,128]{2,1,0:T(8,128)}, u32[]{:S(2)}) copy-start(s32[4,8,128]{2,1,0:T(8,128)} %classes.1) | copy-start | bytes 49156

commit v2 on v1

--- a/solution.py
+++ b/solution.py
@@ -8,6 +8,7 @@
 from jax.sharding import PartitionSpec as P
 
 ITERS = 3
+CHUNKS = 2
 
 
 def gather_nodes(source, row, col):
@@ -23,35 +24,14 @@
 def kernel(
     n_tile,
     n_sec,
-    offsets,
-    flow,
-    conf,
-    owner,
-    flow_row,
-    match_up,
-    match_down,
-    classes,
-    table,
-    pos_out,
-    vel_out,
-    dense,
-    near_other,
-    near_own,
-    crossing,
-    crossed,
-    pos,
-    vel,
-    edge_out,
-    edge_in,
-    near_send,
-    near_recv,
-    cross_send,
-    cross_recv,
-    tile_send,
-    tile_recv,
-    sec_send,
-    sec_recv,
+    *refs,
 ):
+    in_hbm, outs, staged = refs[:9], refs[9:12], refs[12:21]
+    offsets, flow, conf, owner, flow_row, match_up, match_down, classes, table = staged
+    net_out, vel_out, pos_out = outs
+    dense, near_other, near_own, crossing, crossed, pos, vel, edge_out, edge_in = refs[21:30]
+    near_send, near_recv, cross_send, cross_recv = refs[30:34]
+    tile_send, tile_recv, sec_send, sec_recv, load_sem, part_sem = refs[34:]
     comps, secs, rows, cols = offsets.shape
     flows = conf.shape[1]
     half = n_tile // 2
@@ -59,6 +39,23 @@
     s_me = lax.axis_index("sec")
     h, j = t // half, t % half
 
+    chunks = min(CHUNKS, secs)
+    step = secs // chunks
+
+    def load(i):
+        return pltpu.make_async_copy(in_hbm[i], staged[i], load_sem.at[i])
+
+    def load_part(i, s):
+        return pltpu.make_async_copy(in_hbm[i].at[s], staged[i].at[s], part_sem.at[i - 1, s])
+
+    load(3).start()
+    load(4).start()
+    for s in range(secs):
+        load_part(1, s).start()
+        load_part(2, s).start()
+    for i in (0, 5, 6, 7, 8):
+        load(i).start()
+
     barrier = pltpu.get_barrier_semaphore()
     for d in range(1, n_tile):
         pl.semaphore_signal(barrier, inc=1, device_id={"tile": (t + d) % n_tile})
@@ -68,16 +65,11 @@
     for d in (1, n_sec - 1):
         pl.semaphore_signal(barrier, inc=1, device_id={"sec": (s_me + d) % n_sec})
 
-    zero = jnp.zeros((rows, cols), jnp.float32)
-    for s in range(secs):
-        for c in range(comps):
-            here = offsets[c, s]
-            pos[0, s + 1, c] = here
-            edge_out[0, 0, c * secs + s : c * secs + s + 1, :] = here[:1]
-            edge_out[0, 1, c * secs + s : c * secs + s + 1, :] = here[rows - 1 :]
-
     key_iota = lax.broadcasted_iota(jnp.int32, (n_tile * rows, flows), 0)
-    for s in range(secs):
+
+    def segment_sums(s):
+        load_part(1, s).wait()
+        load_part(2, s).wait()
         key = owner[s : s + 1, :] * rows + flow_row[s : s + 1, :]
         hit = (jnp.broadcast_to(key, key_iota.shape) == key_iota).astype(jnp.float32)
         hit = hit.astype(jnp.bfloat16)
@@ -93,8 +85,6 @@
             for c in range(comps + 1):
                 dense[o, s, c] = sums[o * rows : (o + 1) * rows, c * cols : (c + 1) * cols]
 
-    pl.semaphore_wait(barrier, n_tile + 1)
-
     def sec_copy(k, up):
         return pltpu.make_async_remote_copy(
             src_ref=pos.at[k, 1 if up else secs],
@@ -113,25 +103,26 @@
             device_id={"tile": t - 1 if up else t + 1},
         )
 
-    def near_copy(d, part):
+    def near_copy(d, part, m):
         to = (j + d) % half
         source = dense.at[(1 - h if part == 0 else h) * half + to]
         landing = near_other if part == 0 else near_own
         return pltpu.make_async_remote_copy(
-            src_ref=source,
-            dst_ref=landing.at[d - 1],
-            send_sem=near_send.at[part, d - 1],
-            recv_sem=near_recv.at[part, d - 1],
+            src_ref=source.at[pl.ds(m * step, step)],
+            dst_ref=landing.at[d - 1, pl.ds(m * step, step)],
+            send_sem=near_send.at[part, d - 1, m],
+            recv_sem=near_recv.at[part, d - 1, m],
             device_id={"tile": h * half + to},
         )
 
-    cross = pltpu.make_async_remote_copy(
-        src_ref=crossing,
-        dst_ref=crossed,
-        send_sem=cross_send,
-        recv_sem=cross_recv,
-        device_id={"tile": (1 - h) * half + j},
-    )
+    def cross_copy(m):
+        return pltpu.make_async_remote_copy(
+            src_ref=crossing.at[pl.ds(m * step, step)],
+            dst_ref=crossed.at[pl.ds(m * step, step)],
+            send_sem=cross_send.at[m],
+            recv_sem=cross_recv.at[m],
+            device_id={"tile": (1 - h) * half + j},
+        )
 
     def start_halo(k):
         pl.when(has_prev)(lambda: sec_copy(k, True).start())
@@ -160,9 +151,24 @@
             tile_copy(k, False).wait_send()
             tile_copy(k, True).wait_recv()
 
-    for d in range(1, half):
-        near_copy(d, 0).start()
+    load(3).wait()
+    load(4).wait()
+    for m in range(chunks):
+        for s in range(m * step, (m + 1) * step):
+            segment_sums(s)
+        if m == 0:
+            pl.semaphore_wait(barrier, n_tile + 1)
+        for d in range(1, half):
+            near_copy(d, 0, m).start()
+    load(0).wait()
+    for s in range(secs):
+        for c in range(comps):
+            here = offsets[c, s]
+            pos[0, s + 1, c] = here
+            edge_out[0, 0, c * secs + s : c * secs + s + 1, :] = here[:1]
+            edge_out[0, 1, c * secs + s : c * secs + s + 1, :] = here[rows - 1 :]
     start_halo(0)
+    zero = jnp.zeros((rows, cols), jnp.float32)
 
     for k in range(ITERS):
 
@@ -184,6 +190,8 @@
         def _():
             edge_in[k, 1] = jnp.zeros(edge_in.shape[2:], jnp.float32)
 
+    for i in (5, 6, 7, 8):
+        load(i).wait()
     row_iota = lax.broadcasted_iota(jnp.int32, (rows, cols), 0)
     col_iota = lax.broadcasted_iota(jnp.int32, (rows, cols), 1)
     k_plane, k_cross = [], []
@@ -191,8 +199,8 @@
         kind = classes[s]
         plane, across = zero, zero
         for class_id in range(table.shape[1]):
-            plane = jnp.where(kind == class_id, table[0, class_id], plane)
-            across = jnp.where(kind == class_id, table[1, class_id], across)
+            plane = jnp.where(kind == class_id, table[0:1, class_id : class_id + 1], plane)
+            across = jnp.where(kind == class_id, table[1:2, class_id : class_id + 1], across)
         k_plane.append(plane)
         k_cross.append(across)
 
@@ -230,22 +238,25 @@
     for k in range(ITERS):
         force = {(s, c): local_force(k, s, c) for s, c in nodes}
         if k == 0:
+            for m in range(chunks):
+                for d in range(1, half):
+                    near_copy(d, 0, m).wait_recv()
+                for s in range(m * step, (m + 1) * step):
+                    for c in range(comps + 1):
+                        total = dense[(1 - h) * half + j, s, c]
+                        for d in range(1, half):
+                            total = total + near_other[d - 1, s, c]
+                        crossing[s, c] = total
+                cross_copy(m).start()
+            for m in range(chunks):
+                for d in range(1, half):
+                    near_copy(d, 1, m).start()
             wait_halo(0)
             force = {(s, c): force[s, c] + halo_force(0, s, c) for s, c in nodes}
-            for d in range(1, half):
-                near_copy(d, 0).wait_recv()
-            for s in range(secs):
-                for c in range(comps + 1):
-                    total = dense[(1 - h) * half + j, s, c]
-                    for d in range(1, half):
-                        total = total + near_other[d - 1, s, c]
-                    crossing[s, c] = total
-            cross.start()
-            for d in range(1, half):
-                near_copy(d, 1).start()
-            for d in range(1, half):
-                near_copy(d, 1).wait_recv()
-            cross.wait_recv()
+            for m in range(chunks):
+                for d in range(1, half):
+                    near_copy(d, 1, m).wait_recv()
+                cross_copy(m).wait_recv()
             flow_push, flow_hold = {}, {}
             for s in range(secs):
                 sums = []
@@ -264,24 +275,26 @@
         for s, c in nodes:
             here = pos[k, s + 1, c]
             net = force[s, c] + flow_push[s, c] - flow_hold[s] * here
+            if k == ITERS - 1:
+                net_out[c, s] = net
+                vel_out[c, s] = vel[s, c]
+                pos_out[c, s] = here
+                continue
             speed = 0.5 * net if k == 0 else 0.9 * vel[s, c] + 0.5 * net
             moved = here + 0.5 * speed
-            if k < ITERS - 1:
-                vel[s, c] = speed
-                pos[k + 1, s + 1, c] = moved
-                line = c * secs + s
-                edge_out[k + 1, 0, line : line + 1, :] = moved[:1]
-                edge_out[k + 1, 1, line : line + 1, :] = moved[rows - 1 :]
-            else:
-                vel_out[c, s] = speed
-                pos_out[c, s] = moved
+            vel[s, c] = speed
+            pos[k + 1, s + 1, c] = moved
+            line = c * secs + s
+            edge_out[k + 1, 0, line : line + 1, :] = moved[:1]
+            edge_out[k + 1, 1, line : line + 1, :] = moved[rows - 1 :]
         if k < ITERS - 1:
             start_halo(k + 1)
         if k == 0:
-            for d in range(1, half):
-                near_copy(d, 0).wait_send()
-                near_copy(d, 1).wait_send()
-            cross.wait_send()
+            for m in range(chunks):
+                for d in range(1, half):
+                    near_copy(d, 0, m).wait_send()
+                    near_copy(d, 1, m).wait_send()
+                cross_copy(m).wait_send()
 
 
 def shards(n_tile, n_sec, *args):
@@ -295,34 +308,8 @@
     f32 = jnp.float32
     dma = pltpu.SemaphoreType.DMA
     out = jax.ShapeDtypeStruct(offsets.shape, f32)
-    return pl.pallas_call(
-        functools.partial(kernel, n_tile, n_sec),
-        out_shape=(out, out),
-        in_specs=[vmem] * 8 + [pl.BlockSpec(memory_space=pltpu.SMEM)],
-        out_specs=(vmem, vmem),
-        scratch_shapes=[
-            pltpu.VMEM((n_tile,) + block, f32),
-            pltpu.VMEM((half - 1,) + block, f32),
-            pltpu.VMEM((half - 1,) + block, f32),
-            pltpu.VMEM(block, f32),
-            pltpu.VMEM(block, f32),
-            pltpu.VMEM((ITERS, secs + 2, comps, rows, cols), f32),
-            pltpu.VMEM((secs, comps, rows, cols), f32),
-            pltpu.VMEM((ITERS, 2, comps * secs, cols), f32),
-            pltpu.VMEM((ITERS, 2, comps * secs, cols), f32),
-            dma((2, half - 1)),
-            dma((2, half - 1)),
-            dma,
-            dma,
-            dma((ITERS, 2)),
-            dma((ITERS, 2)),
-            dma((ITERS, 2)),
-            dma((ITERS, 2)),
-        ],
-        compiler_params=pltpu.CompilerParams(
-            collective_id=0, has_side_effects=True, vmem_limit_bytes=32 * 1024 * 1024
-        ),
-    )(
+    chunks = min(CHUNKS, secs)
+    operands = (
         offsets,
         flow_tiles.reshape(secs, flows * comps, cols),
         confidence,
@@ -333,6 +320,39 @@
         classes,
         spring_table,
     )
+    net, velocity, position = pl.pallas_call(
+        functools.partial(kernel, n_tile, n_sec),
+        out_shape=(out, out, out),
+        in_specs=[pl.BlockSpec(memory_space=pltpu.HBM)] * 9,
+        out_specs=(vmem, vmem, vmem),
+        scratch_shapes=[pltpu.VMEM(x.shape, x.dtype) for x in operands]
+        + [
+            pltpu.VMEM((n_tile,) + block, f32),
+            pltpu.VMEM((half - 1,) + block, f32),
+            pltpu.VMEM((half - 1,) + block, f32),
+            pltpu.VMEM(block, f32),
+            pltpu.VMEM(block, f32),
+            pltpu.VMEM((ITERS, secs + 2, comps, rows, cols), f32),
+            pltpu.VMEM((secs, comps, rows, cols), f32),
+            pltpu.VMEM((ITERS, 2, comps * secs, cols), f32),
+            pltpu.VMEM((ITERS, 2, comps * secs, cols), f32),
+            dma((2, half - 1, chunks)),
+            dma((2, half - 1, chunks)),
+            dma((chunks,)),
+            dma((chunks,)),
+            dma((ITERS, 2)),
+            dma((ITERS, 2)),
+            dma((ITERS, 2)),
+            dma((ITERS, 2)),
+            dma((9,)),
+            dma((2, secs)),
+        ],
+        compiler_params=pltpu.CompilerParams(
+            collective_id=0, has_side_effects=True, vmem_limit_bytes=63 * 1024 * 1024
+        ),
+    )(*operands)
+    velocity = 0.9 * velocity + 0.5 * net
+    return position + 0.5 * velocity, velocity
 
 
 def solution(mesh):

time: 28.7 us -> 23.5 us (0.82)
  local copies, waits for them, and re-layouts: 6.82 us -> 0 us
  other arithmetic: 0 us -> 1.43 us
  Pallas kernels: 20.7 us -> 21.2 us
    unnamed x20 -> x0, local copies, waits for them, and re-layouts: 6.82 us -> none
    add x0 -> x1, other arithmetic: none -> 1.43 us  [shards(): return (position + 0.5 * velocity, velocity)]
    pallas_call x1, Pallas kernels: 20.7 us -> 21.2 us  [shards(): pl.pallas_call(functools.partial(kernel, n_tile, n_sec), out_shape=(out,...]
where the time goes in v2:
time: 23.5 us; the launch traced here: 23.2 us
  Pallas kernels  21.2 us (90%)
  other arithmetic  1.43 us (6%)
  between operations  0.64 us (3%)
    pallas_call x1, Pallas kernels, shards(): pl.pallas_call(functools.partial(kernel, n_tile, n_sec), out_shape=(out,...  21.2 us
    add x1, other arithmetic, shards(): return (position + 0.5 * velocity, velocity)  1.43 us

profile of v2, /device:TPU:0, one launch (start us, length us, event | category | flops | bytes accessed | tf_op | source)
XLA Modules:
  0.0 23.2 jit_solution(17087219182808125453)
XLA Ops:
  0.6 21.2 %shard_map.104 = (f32[2,4,8,128]{3,2,1,0:T(8,128)}, f32[2,4,8,128]{3,2,1,0:T(8,128)}, f32[2,4,8,128]{3,2,1,0:T(8,128)}) custom-call(f32[2,4,8,128]{3,2,1,0:T(8,128)} %refs_0_.1, f32[4,256,128]{2,1,0:T(8,128)} %bitcast.4, f32[4,128,128]{2,1,0:T(8,128)} %refs_2_.1, s32[4,128]{1,0:T(4,128)} %bitcast.7, s32[4,128]{1,0:T(4,128)} %refs_4_.1, ...), custom_call_target="tpu_custom_call" | custom-call | tf_op jit(solution)/shard_map/pallas_call | solution.py:323
  21.8 1.4 %multiply_add_fusion = (f32[2,4,8,128]{3,2,1,0:T(8,128)}, f32[2,4,8,128]{3,2,1,0:T(8,128)}) fusion(f32[2,4,8,128]{3,2,1,0:T(8,128)} %get-tuple-element.5, f32[2,4,8,128]{3,2,1,0:T(8,128)} %get-tuple-element.7, f32[2,4,8,128]{3,2,1,0:T(8,128)} %get-tuple-element.6), kind=kLoop, calls=%fused_computation | loop fusion | flops 40960 | bytes 163840 | tf_op jit(solution)/shard_map/add | solution.py:355

commit v3 on v2

--- a/solution.py
+++ b/solution.py
@@ -8,7 +8,7 @@
 from jax.sharding import PartitionSpec as P
 
 ITERS = 3
-CHUNKS = 2
+CHUNKS = 1
 
 
 def gather_nodes(source, row, col):
@@ -57,13 +57,27 @@
         load(i).start()
 
     barrier = pltpu.get_barrier_semaphore()
-    for d in range(1, n_tile):
-        pl.semaphore_signal(barrier, inc=1, device_id={"tile": (t + d) % n_tile})
     has_prev, has_next = s_me > 0, s_me < n_sec - 1
     has_left, has_right = t > 0, t < n_tile - 1
 
-    for d in (1, n_sec - 1):
-        pl.semaphore_signal(barrier, inc=1, device_id={"sec": (s_me + d) % n_sec})
+    for d in range(1, half):
+        pl.semaphore_signal(barrier, inc=1, device_id={"tile": h * half + (j + d) % half})
+    pl.semaphore_signal(barrier, inc=1, device_id={"tile": (1 - h) * half + j})
+    over_right = jnp.logical_and(t == half - 1, half > 1)
+    over_left = jnp.logical_and(t == half, half > 1)
+
+    def greet(there, partner):
+        @pl.when(there)
+        def _():
+            pl.semaphore_signal(barrier, inc=1, device_id=partner)
+
+    greet(has_prev, {"sec": s_me - 1})
+    greet(has_next, {"sec": s_me + 1})
+    greet(over_right, {"tile": t + 1})
+    greet(over_left, {"tile": t - 1})
+    partners = half
+    for there in (has_prev, has_next, over_right, over_left):
+        partners = partners + there.astype(jnp.int32)
 
     key_iota = lax.broadcasted_iota(jnp.int32, (n_tile * rows, flows), 0)
 
@@ -125,31 +139,34 @@
         )
 
     def start_halo(k):
+        pl.when(has_left)(lambda: tile_copy(k, True).start())
+        pl.when(has_right)(lambda: tile_copy(k, False).start())
         pl.when(has_prev)(lambda: sec_copy(k, True).start())
         pl.when(has_next)(lambda: sec_copy(k, False).start())
-        pl.when(has_left)(lambda: tile_copy(k, True).start())
-        pl.when(has_right)(lambda: tile_copy(k, False).start())
-
-    def wait_halo(k):
+
+    def wait_sec(k):
         @pl.when(has_prev)
         def _():
-            sec_copy(k, True).wait_send()
             sec_copy(k, False).wait_recv()
 
         @pl.when(has_next)
         def _():
-            sec_copy(k, False).wait_send()
             sec_copy(k, True).wait_recv()
 
+    def wait_tile(k):
         @pl.when(has_left)
         def _():
-            tile_copy(k, True).wait_send()
             tile_copy(k, False).wait_recv()
 
         @pl.when(has_right)
         def _():
-            tile_copy(k, False).wait_send()
             tile_copy(k, True).wait_recv()
+
+    def wait_sent(k):
+        pl.when(has_left)(lambda: tile_copy(k, True).wait_send())
+        pl.when(has_right)(lambda: tile_copy(k, False).wait_send())
+        pl.when(has_prev)(lambda: sec_copy(k, True).wait_send())
+        pl.when(has_next)(lambda: sec_copy(k, False).wait_send())
 
     load(3).wait()
     load(4).wait()
@@ -157,7 +174,7 @@
         for s in range(m * step, (m + 1) * step):
             segment_sums(s)
         if m == 0:
-            pl.semaphore_wait(barrier, n_tile + 1)
+            pl.semaphore_wait(barrier, partners)
         for d in range(1, half):
             near_copy(d, 0, m).start()
     load(0).wait()
@@ -222,18 +239,27 @@
             force = force + k_cross[s] * pulled(k, s, c, False)
         return force
 
-    def halo_force(k, s, c):
+    def sec_force(k, s, c):
+        if s == secs - 1:
+            force[s, c] = force[s, c] + k_cross[s] * pulled(k, s, c, True)
+        if s == 0:
+            force[s, c] = force[s, c] + k_cross[s] * pulled(k, s, c, False)
+
+    def tile_force(k, s, c):
         line = c * secs + s
         north = jnp.where(row_iota == 0, edge_in[k, 0, line : line + 1, :], 0.0)
         south = jnp.where(row_iota == rows - 1, edge_in[k, 1, line : line + 1, :], 0.0)
-        force = k_plane[s] * (north + south)
-        if s == secs - 1:
-            force = force + k_cross[s] * pulled(k, s, c, True)
-        if s == 0:
-            force = force + k_cross[s] * pulled(k, s, c, False)
-        return force
+        force[s, c] = force[s, c] + k_plane[s] * (north + south)
 
     nodes = [(s, c) for s in [0, secs - 1] + list(range(1, secs - 1)) for c in range(comps)]
+
+    def halo_force(k):
+        wait_sec(k)
+        for s, c in nodes:
+            sec_force(k, s, c)
+        wait_tile(k)
+        for s, c in nodes:
+            tile_force(k, s, c)
 
     for k in range(ITERS):
         force = {(s, c): local_force(k, s, c) for s, c in nodes}
@@ -251,8 +277,7 @@
             for m in range(chunks):
                 for d in range(1, half):
                     near_copy(d, 1, m).start()
-            wait_halo(0)
-            force = {(s, c): force[s, c] + halo_force(0, s, c) for s, c in nodes}
+            halo_force(0)
             for m in range(chunks):
                 for d in range(1, half):
                     near_copy(d, 1, m).wait_recv()
@@ -270,11 +295,13 @@
                 for c in range(comps):
                     flow_push[s, c] = sums[c] * scale
         else:
-            wait_halo(k)
-            force = {(s, c): force[s, c] + halo_force(k, s, c) for s, c in nodes}
+            force = {(s, c): force[s, c] + flow_push[s, c] - flow_hold[s] * pos[k, s + 1, c] for s, c in nodes}
+            halo_force(k)
         for s, c in nodes:
             here = pos[k, s + 1, c]
-            net = force[s, c] + flow_push[s, c] - flow_hold[s] * here
+            net = force[s, c]
+            if k == 0:
+                net = net + flow_push[s, c] - flow_hold[s] * here
             if k == ITERS - 1:
                 net_out[c, s] = net
                 vel_out[c, s] = vel[s, c]
@@ -289,6 +316,7 @@
             edge_out[k + 1, 1, line : line + 1, :] = moved[rows - 1 :]
         if k < ITERS - 1:
             start_halo(k + 1)
+        wait_sent(k)
         if k == 0:
             for m in range(chunks):
                 for d in range(1, half):
@@ -307,7 +335,6 @@
     vmem = pl.BlockSpec(memory_space=pltpu.VMEM)
     f32 = jnp.float32
     dma = pltpu.SemaphoreType.DMA
-    out = jax.ShapeDtypeStruct(offsets.shape, f32)
     chunks = min(CHUNKS, secs)
     operands = (
         offsets,
@@ -322,7 +349,7 @@
     )
     net, velocity, position = pl.pallas_call(
         functools.partial(kernel, n_tile, n_sec),
-        out_shape=(out, out, out),
+        out_shape=(pltpu.VMEM(offsets.shape, f32),) * 3,
         in_specs=[pl.BlockSpec(memory_space=pltpu.HBM)] * 9,
         out_specs=(vmem, vmem, vmem),
         scratch_shapes=[pltpu.VMEM(x.shape, x.dtype) for x in operands]

time: 23.5 us -> 20.9 us (0.89)
  Pallas kernels: 21.2 us -> 19.5 us
  other arithmetic: 1.43 us -> 0.64 us
    pallas_call x1, Pallas kernels: 21.2 us -> 19.5 us  [shards(): pl.pallas_call(functools.partial(kernel, n_tile, n_sec), out_shape=(pltpu...]
    add x1, other arithmetic: 1.43 us -> 0.64 us  [shards(): return (position + 0.5 * velocity, velocity)]
where the time goes in v3:
time: 20.9 us; the launch traced here: 20.8 us
  Pallas kernels  19.5 us (93%)
  other arithmetic  0.64 us (3%)
  between operations  0.64 us (3%)
    pallas_call x1, Pallas kernels, shards(): pl.pallas_call(functools.partial(kernel, n_tile, n_sec), out_shape=(pltpu...  19.5 us
    add x1, other arithmetic, shards(): return (position + 0.5 * velocity, velocity)  0.64 us

profile of v3, /device:TPU:0, one launch (start us, length us, event | category | flops | bytes accessed | tf_op | source)
XLA Modules:
  0.0 20.8 jit_solution(12327575764334504355)
XLA Ops:
  0.6 19.5 %shard_map.104 = (f32[2,4,8,128]{3,2,1,0:T(8,128)S(1)}, f32[2,4,8,128]{3,2,1,0:T(8,128)S(1)}, f32[2,4,8,128]{3,2,1,0:T(8,128)S(1)}) custom-call(f32[2,4,8,128]{3,2,1,0:T(8,128)} %refs_0_.1, f32[4,256,128]{2,1,0:T(8,128)} %bitcast.4, f32[4,128,128]{2,1,0:T(8,128)} %refs_2_.1, s32[4,128]{1,0:T(4,128)} %bitcast.7, s32[4,128]{1,0:T(4,128)} %refs_4_.1, ...), custom_call_target="tpu_custom_call" | custom-call | tf_op jit(solution)/shard_map/pallas_call | solution.py:350
  20.2 0.6 %multiply_add_fusion = (f32[2,4,8,128]{3,2,1,0:T(8,128)}, f32[2,4,8,128]{3,2,1,0:T(8,128)}) fusion(f32[2,4,8,128]{3,2,1,0:T(8,128)S(1)} %get-tuple-element.5, f32[2,4,8,128]{3,2,1,0:T(8,128)S(1)} %get-tuple-element.7, f32[2,4,8,128]{3,2,1,0:T(8,128)S(1)} %get-tuple-element.6), kind=kLoop, calls=%fused_computation | loop fusion | flops 40960 | bytes 163840 | tf_op jit(solution)/shard_map/add | solution.py:382

commit v4 on v3

--- a/solution.py
+++ b/solution.py
@@ -31,7 +31,7 @@
     net_out, vel_out, pos_out = outs
     dense, near_other, near_own, crossing, crossed, pos, vel, edge_out, edge_in = refs[21:30]
     near_send, near_recv, cross_send, cross_recv = refs[30:34]
-    tile_send, tile_recv, sec_send, sec_recv, load_sem, part_sem = refs[34:]
+    tile_send, tile_recv, sec_send, sec_recv, load_sem = refs[34:]
     comps, secs, rows, cols = offsets.shape
     flows = conf.shape[1]
     half = n_tile // 2
@@ -45,16 +45,10 @@
     def load(i):
         return pltpu.make_async_copy(in_hbm[i], staged[i], load_sem.at[i])
 
-    def load_part(i, s):
-        return pltpu.make_async_copy(in_hbm[i].at[s], staged[i].at[s], part_sem.at[i - 1, s])
-
     load(3).start()
     load(4).start()
-    for s in range(secs):
-        load_part(1, s).start()
-        load_part(2, s).start()
-    for i in (0, 5, 6, 7, 8):
-        load(i).start()
+    load(1).start()
+    load(2).start()
 
     barrier = pltpu.get_barrier_semaphore()
     has_prev, has_next = s_me > 0, s_me < n_sec - 1
@@ -82,8 +76,6 @@
     key_iota = lax.broadcasted_iota(jnp.int32, (n_tile * rows, flows), 0)
 
     def segment_sums(s):
-        load_part(1, s).wait()
-        load_part(2, s).wait()
         key = owner[s : s + 1, :] * rows + flow_row[s : s + 1, :]
         hit = (jnp.broadcast_to(key, key_iota.shape) == key_iota).astype(jnp.float32)
         hit = hit.astype(jnp.bfloat16)
@@ -168,14 +160,16 @@
         pl.when(has_prev)(lambda: sec_copy(k, True).wait_send())
         pl.when(has_next)(lambda: sec_copy(k, False).wait_send())
 
-    load(3).wait()
-    load(4).wait()
+    for i in (0, 5, 6, 7, 8):
+        load(i).start()
+    for i in (3, 4, 1, 2):
+        load(i).wait()
     for m in range(chunks):
         for s in range(m * step, (m + 1) * step):
             segment_sums(s)
         if m == 0:
             pl.semaphore_wait(barrier, partners)
-        for d in range(1, half):
+        for d in list(range(1, half, 2)) + list(range(2, half, 2)):
             near_copy(d, 0, m).start()
     load(0).wait()
     for s in range(secs):
@@ -372,7 +366,6 @@
             dma((ITERS, 2)),
             dma((ITERS, 2)),
             dma((9,)),
-            dma((2, secs)),
         ],
         compiler_params=pltpu.CompilerParams(
             collective_id=0, has_side_effects=True, vmem_limit_bytes=63 * 1024 * 1024

time: 20.9 us -> 20.8 us (level)
  no operation moved by 1% of the time
where the time goes in v4:
time: 20.8 us; the launch traced here: 20.7 us
  Pallas kernels  19.4 us (93%)
  other arithmetic  0.64 us (3%)
  between operations  0.64 us (3%)
    pallas_call x1, Pallas kernels, shards(): pl.pallas_call(functools.partial(kernel, n_tile, n_sec), out_shape=(pltpu...  19.4 us
    add x1, other arithmetic, shards(): return (position + 0.5 * velocity, velocity)  0.64 us

profile of v4, /device:TPU:0, one launch (start us, length us, event | category | flops | bytes accessed | tf_op | source)
XLA Modules:
  0.0 20.7 jit_solution(13006219923144002296)
XLA Ops:
  0.6 19.4 %shard_map.104 = (f32[2,4,8,128]{3,2,1,0:T(8,128)S(1)}, f32[2,4,8,128]{3,2,1,0:T(8,128)S(1)}, f32[2,4,8,128]{3,2,1,0:T(8,128)S(1)}) custom-call(f32[2,4,8,128]{3,2,1,0:T(8,128)} %refs_0_.1, f32[4,256,128]{2,1,0:T(8,128)} %bitcast.4, f32[4,128,128]{2,1,0:T(8,128)} %refs_2_.1, s32[4,128]{1,0:T(4,128)} %bitcast.7, s32[4,128]{1,0:T(4,128)} %refs_4_.1, ...), custom_call_target="tpu_custom_call" | custom-call | tf_op jit(solution)/shard_map/pallas_call | solution.py:344
  20.0 0.6 %multiply_add_fusion = (f32[2,4,8,128]{3,2,1,0:T(8,128)}, f32[2,4,8,128]{3,2,1,0:T(8,128)}) fusion(f32[2,4,8,128]{3,2,1,0:T(8,128)S(1)} %get-tuple-element.5, f32[2,4,8,128]{3,2,1,0:T(8,128)S(1)} %get-tuple-element.7, f32[2,4,8,128]{3,2,1,0:T(8,128)S(1)} %get-tuple-element.6), kind=kLoop, calls=%fused_computation | loop fusion | flops 40960 | bytes 163840 | tf_op jit(solution)/shard_map/add | solution.py:375

commit v5 on v4

--- a/solution.py
+++ b/solution.py
@@ -130,9 +130,11 @@
             device_id={"tile": (1 - h) * half + j},
         )
 
-    def start_halo(k):
+    def start_tile(k):
         pl.when(has_left)(lambda: tile_copy(k, True).start())
         pl.when(has_right)(lambda: tile_copy(k, False).start())
+
+    def start_sec(k):
         pl.when(has_prev)(lambda: sec_copy(k, True).start())
         pl.when(has_next)(lambda: sec_copy(k, False).start())
 
@@ -178,7 +180,8 @@
             pos[0, s + 1, c] = here
             edge_out[0, 0, c * secs + s : c * secs + s + 1, :] = here[:1]
             edge_out[0, 1, c * secs + s : c * secs + s + 1, :] = here[rows - 1 :]
-    start_halo(0)
+    start_tile(0)
+    start_sec(0)
     zero = jnp.zeros((rows, cols), jnp.float32)
 
     for k in range(ITERS):
@@ -291,6 +294,7 @@
         else:
             force = {(s, c): force[s, c] + flow_push[s, c] - flow_hold[s] * pos[k, s + 1, c] for s, c in nodes}
             halo_force(k)
+        later = {}
         for s, c in nodes:
             here = pos[k, s + 1, c]
             net = force[s, c]
@@ -303,13 +307,15 @@
                 continue
             speed = 0.5 * net if k == 0 else 0.9 * vel[s, c] + 0.5 * net
             moved = here + 0.5 * speed
-            vel[s, c] = speed
-            pos[k + 1, s + 1, c] = moved
+            later[s, c] = (speed, moved)
             line = c * secs + s
             edge_out[k + 1, 0, line : line + 1, :] = moved[:1]
             edge_out[k + 1, 1, line : line + 1, :] = moved[rows - 1 :]
         if k < ITERS - 1:
-            start_halo(k + 1)
+            start_tile(k + 1)
+            for s, c in nodes:
+                vel[s, c], pos[k + 1, s + 1, c] = later[s, c]
+            start_sec(k + 1)
         wait_sent(k)
         if k == 0:
             for m in range(chunks):

time: 20.8 us -> 20.8 us (level)
  no operation moved by 1% of the time
where the time goes in v5:
time: 20.8 us; the launch traced here: 20.7 us
  Pallas kernels  19.4 us (93%)
  other arithmetic  0.64 us (3%)
  between operations  0.64 us (3%)
    pallas_call x1, Pallas kernels, shards(): pl.pallas_call(functools.partial(kernel, n_tile, n_sec), out_shape=(pltpu...  19.4 us
    add x1, other arithmetic, shards(): return (position + 0.5 * velocity, velocity)  0.64 us

profile of v5, /device:TPU:0, one launch (start us, length us, event | category | flops | bytes accessed | tf_op | source)
XLA Modules:
  0.0 20.7 jit_solution(236611293040124350)
XLA Ops:
  0.6 19.4 %shard_map.104 = (f32[2,4,8,128]{3,2,1,0:T(8,128)S(1)}, f32[2,4,8,128]{3,2,1,0:T(8,128)S(1)}, f32[2,4,8,128]{3,2,1,0:T(8,128)S(1)}) custom-call(f32[2,4,8,128]{3,2,1,0:T(8,128)} %refs_0_.1, f32[4,256,128]{2,1,0:T(8,128)} %bitcast.4, f32[4,128,128]{2,1,0:T(8,128)} %refs_2_.1, s32[4,128]{1,0:T(4,128)} %bitcast.7, s32[4,128]{1,0:T(4,128)} %refs_4_.1, ...), custom_call_target="tpu_custom_call" | custom-call | tf_op jit(solution)/shard_map/pallas_call | solution.py:350
  20.0 0.6 %multiply_add_fusion = (f32[2,4,8,128]{3,2,1,0:T(8,128)}, f32[2,4,8,128]{3,2,1,0:T(8,128)}) fusion(f32[2,4,8,128]{3,2,1,0:T(8,128)S(1)} %get-tuple-element.5, f32[2,4,8,128]{3,2,1,0:T(8,128)S(1)} %get-tuple-element.7, f32[2,4,8,128]{3,2,1,0:T(8,128)S(1)} %get-tuple-element.6), kind=kLoop, calls=%fused_computation | loop fusion | flops 40960 | bytes 163840 | tf_op jit(solution)/shard_map/add | solution.py:381
